TPU v7x, 128 devices: a whole 4x4x4 slice. The times are simulated.
128 devices in a mesh: lat: 8 (over z, core), lon: 16 (over x, y).
Axes of the slice: x: 4, y: 4, z: 4, core: 2. Of those that a mesh axis runs over, the one named last changes fastest.
Arguments:
- grid_latent: bfloat16 [64, 2048, 512], P('lat', 'lon'), may hold values from -6 to 6
- mesh_latent: bfloat16 [8, 16, 320, 512], P('lat', 'lon'), may hold values from -6 to 6
- edge_latent: bfloat16 [8, 16, 2560, 512], P('lat', 'lon'), may hold values from -6 to 6
- g2m_src: int32 [8, 16, 1536], P('lat', 'lon'), may hold values from 0 to 1583, as said below
- g2m_dst: int32 [8, 16, 1536], P('lat', 'lon'), may hold values from 0 to 319
- g2m_count: int32 [8, 16], P('lat', 'lon'), may hold values from 577 to 1536, as said below
- mesh_src: int32 [8, 16, 2560], P('lat', 'lon'), may hold values from 0 to 4927, as said below
- mesh_dst: int32 [8, 16, 2560], P('lat', 'lon'), may hold values from 0 to 319
- m2g_src: int32 [3, 64, 2048], P(None, 'lat', 'lon'), may hold values from 0 to 2879, as said below
- weights_in: bfloat16 [18, 512, 512], replicated, may hold values from -0.25 to 0.25
- weights_out: bfloat16 [8, 512, 512], replicated, may hold values from -0.25 to 0.25
- gains: float32 [8, 512], replicated, may hold values from 0.25 to 1.75
Outputs:
- grid_out: bfloat16 [64, 2048, 512], P('lat', 'lon')
Inputs may be any that keep to these rules, and one draw needn't show every extreme that they name: `g2m_src`: live slots read only cells of the widened tile that lie inside the latitude range of the grid (no cell beyond a pole). `g2m_count`: the first and last latitude bands fill all 1536 slots. `mesh_src`: A sender below 2880 is node j of nine-patch block k (index k * 320 + j); for k other than 4 the block lies inside the latitude range and j < 64. A sender of 2880 or more is a coarse node: the last 16 nodes of every patch in patch order. `m2g_src`: index k * 320 + j into the nine patches around the cell's tile; for k other than 4 the patch lies inside the latitude range and j < 64.
All inputs are finite; a program needn't handle non-finite values.
Results may differ from a plain program's by a relative error of at most 0.017.
Values may be sent and summed in bfloat16 or wider, within the bound.
A program may use at most 128 MiB of HBM per device.

v0:
```python
import jax
import jax.numpy as jnp
from jax import lax
from jax.experimental import pallas as pl
from jax.experimental.pallas import tpu as pltpu
from jax.sharding import PartitionSpec as P

L = 512
ROWS = 8
COLS = 128
MESH = 320
BORDER = 64
COARSE = 16
EDGE = 2560
G2M = 1536
ROUNDS = 2
CELLS = ROWS * COLS
N_LAT = 8
N_LON = 16
OUT = 18

NORTH, SOUTH, STRIPS = 1408, 1664, 1920
GRID_ROWS = 1632
NEAR_AT, COARSE_AT, WIDE = 640, 1152, 3200
DEC_OWN, DEC_WIDE = 384, 896

TILE = 512
EPSILON = 1e-05
F32 = jnp.float32
BF16 = jnp.bfloat16
NEIGHBOURS = [(p, q) for p in (-1, 0, 1) for q in (-1, 0, 1) if (p, q) != (0, 0)]
FAR_FIRST = sorted(
    ((i, j) for i in range(4) for j in range(4) if (i, j) != (0, 0)),
    key=lambda d: -min(d[0], 4 - d[0]) - min(d[1], 4 - d[1]),
)
XY = [(i, j, 0) for i, j in FAR_FIRST]
YZ = [(0, i, j) for i, j in FAR_FIRST]
PARTS = [(pl.ds(0, 256), "z", XY), (pl.ds(256, 256), "x", YZ)]


def tiles(count):
    return [pl.ds(t * TILE, TILE) for t in range(count // TILE)]


def dot(a, b):
    return jnp.dot(a, b, preferred_element_type=F32)


def hidden(before):
    half = 0.5 * before
    return (half + half * jnp.tanh(half)).astype(BF16)


def norm(result, gain):
    centre = jnp.sum(result, axis=-1, keepdims=True) * (1.0 / L)
    centred = result - centre
    spread = jnp.sum(centred * centred, axis=-1, keepdims=True) * (1.0 / L)
    return centred * lax.rsqrt(spread + EPSILON) * gain


def ones_where(mask):
    return jnp.where(mask, 1.0, 0.0).astype(BF16)


def short(value):
    return value.astype(jnp.int32).astype(jnp.int16)


def ones_where_short(mask):
    return jnp.where(mask, jnp.ones((), BF16), jnp.zeros((), BF16))


def steps_below(value, size, count):
    index = jnp.zeros_like(value)
    for step in range(1, count):
        index = index + jnp.where(value >= step * size, 1, 0)
    return index


def near_slot(source, own_at, near_at):
    block = steps_below(source, MESH, 9)
    row = source - block * MESH
    slot = block - jnp.where(block > 4, 1, 0)
    return jnp.where(block == 4, own_at + row, near_at + slot * BORDER + row)


def grid_slot(cell):
    r = steps_below(cell, COLS + 4, ROWS + 4)
    c = cell - r * (COLS + 4)
    north, south = r < 2, r >= ROWS + 2
    west, east = c < 2, c >= COLS + 2
    inside = (r - 2) * COLS + c - 2
    inside = jnp.where(north, NORTH + r * COLS + c - 2, inside)
    inside = jnp.where(south, SOUTH + (r - (ROWS + 2)) * COLS + c - 2, inside)
    strip = jnp.where(north, 2, jnp.where(south, 4, 0)) + jnp.where(east, 1, 0)
    strip_row = jnp.where(north, r + ROWS - 2, jnp.where(south, r - (ROWS + 2), r - 2))
    strip_col = jnp.where(east, c - (COLS + 2), c)
    side = STRIPS + strip * 16 + strip_row * 2 + strip_col
    return jnp.where(west | east, side, inside)


def edge_slot(source, core):
    far = source - 9 * MESH
    other = ((far >> 8) + core) & 1
    coarse = COARSE_AT + other * 1024 + (far >> 9) * 256 + (far & 255)
    return jnp.where(far >= 0, coarse, near_slot(source, 0, NEAR_AT))


def kernel(
    grid, mesh_in, edge_in, g2m_src, g2m_dst, g2m_count, mesh_src, mesh_dst, m2g_src,
    weights_in, weights_out, gains, out,
    w, cells, table, edges, acc, pick, place, coarse, near, proj, message, mesh_now, own_part, strips, square,
    local_sem, send_sem, recv_sem,
):
    lat, lon = lax.axis_index("lat"), lax.axis_index("lon")
    z, core = lax.div(lat, 2), lax.rem(lat, 2)
    x, y = lax.div(lon, 4), lax.rem(lon, 4)
    counts = {"local": 0, "remote": 0}

    def local(src, dst):
        i = counts["local"]
        counts["local"] += 1
        copy = pltpu.make_async_copy(src, dst, local_sem.at[i])
        copy.start()
        return copy

    def remote(src, dst, device):
        i = counts["remote"]
        counts["remote"] += 1
        copy = pltpu.make_async_remote_copy(
            src_ref=src, dst_ref=dst, send_sem=send_sem.at[i], recv_sem=recv_sem.at[i],
            device_id=device, device_id_type=pl.DeviceIdType.MESH,
        )
        copy.start()
        return copy

    def beside(p, q):
        return (lax.rem(lat + (p + N_LAT), N_LAT), lax.rem(lon + (q + N_LON), N_LON))

    def chip(dx, dy, dz):
        return (lax.rem(z + dz, 4) * 2 + core, lax.rem(x + dx, 4) * 4 + lax.rem(y + dy, 4))

    sibling = (z * 2 + (1 - core), lon)

    got_grid = local(grid, cells.at[pl.ds(0, CELLS)])
    got_weights = []
    for first, many, first_out, many_out in ((0, 4, 0, 2), (4, 5, 2, 2), (9, 5, 4, 2), (14, 4, 6, 2)):
        got_weights.append((
            local(weights_in.at[pl.ds(first, many)], w.at[pl.ds(first, many)]),
            local(weights_out.at[pl.ds(first_out, many_out)], w.at[pl.ds(OUT + first_out, many_out)]),
        ))
        if first == 0:
            got_edges = local(edge_in, edges)

    barrier = pltpu.get_barrier_semaphore()
    peers = [beside(p, q) for p, q in NEIGHBOURS] + [chip(*d) for d in sorted(set(XY + YZ))] + [sibling]
    for peer in peers:
        pl.semaphore_signal(barrier, inc=1, device_id=peer, device_id_type=pl.DeviceIdType.MESH)

    got_grid.wait()
    i = lax.broadcasted_iota(jnp.int32, (16, COLS), 0)
    j = lax.broadcasted_iota(jnp.int32, (16, COLS), 1)
    for side, first, shift in ((0, COLS - 16, 14), (1, 0, 0)):
        rim = jnp.concatenate([cells[r * COLS + first : r * COLS + first + 16] for r in range(ROWS)], axis=0)
        wanted = (i >> 1) * 16 + shift + (i & 1)
        strips[side] = dot(ones_where(j == wanted), rim).astype(BF16)

    pl.semaphore_wait(barrier, len(peers))
    halo = [
        remote(grid.at[pl.ds(CELLS - 256, 256)], cells.at[pl.ds(CELLS, 256)], beside(1, 0)),
        remote(grid.at[pl.ds(0, 256)], cells.at[pl.ds(CELLS + 256, 256)], beside(-1, 0)),
    ]
    for side, q in ((0, 1), (1, -1)):
        for place_at, p in ((0, 0), (2, 1), (4, -1)):
            to = CELLS + 512 + (place_at + side) * 16
            halo.append(remote(strips.at[side], cells.at[pl.ds(to, 16)], beside(p, q)))

    lanes = lax.broadcasted_iota(jnp.int32, (128, 128), 1).astype(jnp.int16)
    nodes = lax.broadcasted_iota(jnp.int32, (MESH, 128), 0)

    def stacked(ref):
        square[...] = jnp.zeros_like(square)
        many = ref.shape[1] // 128
        for t in range(many):
            square[t : t + 1, :] = ref[0:1, t * 128 : t * 128 + 128].astype(F32)
        return square[...].astype(jnp.int32), many

    def columns(index, many, at):
        turned = index.astype(F32).T
        for t in range(many):
            acc[t * 128 : t * 128 + 128, at : at + 128] = jnp.broadcast_to(turned[:, t : t + 1], (128, 128))

    source, many = stacked(g2m_src)
    columns(grid_slot(source), many, 0)
    target, many = stacked(g2m_dst)
    columns(target + CELLS, many, 128)

    @pl.loop(0, G2M // 128)
    def _(t):
        rows = pl.ds(pl.multiple_of(t * 128, 128), 128)
        first, second = short(acc[rows, 0:128]), short(acc[rows, 128:256])
        for chunk in range(16):
            ids = lanes + jnp.int16(chunk * 128)
            mask = (second if 8 <= chunk < 11 else first) == ids
            pick[rows, chunk * 128 : chunk * 128 + 128] = ones_where_short(mask)

    live = g2m_count[...]
    lane = lax.broadcasted_iota(jnp.int32, (1, 128), 1)
    for t in range(G2M // 128):
        target = jnp.where(lane + t * 128 < live, g2m_dst[0:1, t * 128 : t * 128 + 128], -1)
        place[:, EDGE + t * 128 : EDGE + t * 128 + 128] = ones_where(nodes == target)

    got_weights[0][0].wait()
    got_weights[0][1].wait()

    @pl.loop(0, CELLS // TILE)
    def _(t):
        rows = pl.ds(pl.multiple_of(t * TILE, TILE), TILE)
        table[rows, :] = dot(cells[rows, :], w[0]).astype(BF16)

    table[CELLS : CELLS + MESH] = dot(mesh_in[...], w[1]).astype(BF16)
    table[CELLS + MESH : NORTH] = jnp.zeros((NORTH - CELLS - MESH, L), BF16)
    table[NORTH + 608 :] = jnp.zeros((2048 - NORTH - 608, L), BF16)
    own_part[...] = dot(mesh_in[...], w[2])

    @pl.loop(0, G2M // TILE)
    def _(t):
        rows = pl.ds(pl.multiple_of(t * TILE, TILE), TILE)
        acc[rows, :] = dot(pick[rows, 0:NORTH], table[0:NORTH])

    for copy in halo:
        copy.wait_recv()
    table[NORTH : NORTH + 608] = dot(cells[CELLS:GRID_ROWS], w[0]).astype(BF16)

    for rows in tiles(G2M):
        before = acc[rows, :] + dot(pick[rows, NORTH:2048], table[NORTH:2048])
        message[rows, :] = norm(dot(hidden(before), w[OUT]), gains[0:1, :]).astype(BF16)

    def new_nodes(old, self_part, totals, second, k):
        before = self_part + dot(totals.astype(BF16), w[second])
        return (old.astype(F32) + norm(dot(hidden(before), w[OUT + k]), gains[k : k + 1, :])).astype(BF16)

    def update_encoded(a, b):
        totals = dot(place[a:b, EDGE : EDGE + G2M], message[...])
        mesh_now[a:b] = new_nodes(mesh_in[a:b], own_part[a:b], totals, 3, 1)

    def update_round(r):
        def update(a, b):
            totals = dot(place[a:b, 0:EDGE], edges[...])
            mesh_now[a:b] = new_nodes(mesh_now[a:b], own_part[a:b], totals, 8 + 5 * r, 3 + 2 * r)

        return update

    sent = list(halo)

    def send_near(r):
        copies = []
        for slot, (p, q) in enumerate(NEIGHBOURS):
            copies.append(remote(proj.at[r, pl.ds(0, BORDER)], near.at[r, slot], beside(-p, -q)))
        sent.extend(copies)
        return copies

    def plane(r, part, axis, d):
        here = lax.rem({"x": x, "z": z}[axis] + (4 - d), 4)
        if axis == "z":
            return coarse.at[r, 0, here, :, :, :, part]
        return coarse.at[r, 0, :, here, :, :, part]

    update = update_encoded
    for r in range(ROUNDS):
        first = 4 + 5 * r
        got_weights[1 + r][0].wait()
        got_weights[1 + r][1].wait()
        update(MESH - COARSE, MESH)
        coarse[r, 0, z, x, y] = dot(mesh_now[MESH - COARSE : MESH], w[first + 1]).astype(BF16)
        arriving = []
        for part, axis, offsets in PARTS:
            ref = coarse.at[r, 0, z, x, y, :, part]
            arriving.append([remote(ref, ref, chip(*d)) for d in offsets])
            sent.extend(arriving[-1])
        update(0, MESH - COARSE)
        proj[r, 0:MESH] = dot(mesh_now[...], w[first + 1]).astype(BF16)
        got_near = send_near(r)
        proj[r, MESH : 2 * MESH] = dot(mesh_now[...], w[first + 2]).astype(BF16)
        own_part[...] = dot(mesh_now[...], w[first + 3])

        if r == 0:
            got_edges.wait()
            source, many = stacked(mesh_src)
            columns(edge_slot(source, core), many, 0)
            target, many = stacked(mesh_dst)
            columns(target + MESH, many, 128)

        across = []

        def second_stage():
            moving = []
            for k, (part, axis, offsets) in enumerate(PARTS):
                for copy in arriving[k]:
                    copy.wait_recv()
                ref = plane(r, part, axis, 0)
                moving.append([
                    remote(ref, ref, chip(**{"dx": 0, "dy": 0, "dz": 0, "d" + axis: d})) for d in (1, 2, 3)
                ])
                sent.extend(moving[-1])
            for part, axis, offsets in PARTS:
                across.append(forward(part, axis, 0))
            return moving

        def forward(part, axis, d):
            here = lax.rem({"x": x, "z": z}[axis] + (4 - d), 4)
            if axis == "z":
                return remote(
                    coarse.at[r, 0, here, :, :, :, part], coarse.at[r, 1, here, :, :, :, part], sibling
                )
            return remote(
                coarse.at[r, 0, :, here, :, :, part], coarse.at[r, 1, :, here, :, :, part], sibling
            )

        if r == 0:
            moving = second_stage()

            @pl.loop(0, EDGE // 128)
            def _(t):
                rows = pl.ds(pl.multiple_of(t * 128, 128), 128)
                one, two = short(acc[rows, 0:128]), short(acc[rows, 128:256])
                for chunk in range(WIDE // 128):
                    ids = lanes + jnp.int16(chunk * 128)
                    if chunk in (3, 4):
                        mask = two == ids
                    elif chunk == 2:
                        mask = (one == ids) | (two == ids)
                    else:
                        mask = one == ids
                    pick[rows, chunk * 128 : chunk * 128 + 128] = ones_where_short(mask)

            for t in range(EDGE // 128):
                place[:, t * 128 : t * 128 + 128] = ones_where(nodes == mesh_dst[0:1, t * 128 : t * 128 + 128])

        if r == 0:
            for copy in got_near:
                copy.wait_recv()
            for rows in tiles(EDGE):
                acc[rows, :] = (
                    dot(edges[rows, :], w[first])
                    + dot(pick[rows, 0:NEAR_AT], proj[r])
                    + dot(pick[rows, NEAR_AT:COARSE_AT], near[r].reshape(8 * BORDER, L))
                )
        else:
            for rows in tiles(EDGE):
                acc[rows, :] = dot(edges[rows, :], w[first]) + dot(pick[rows, 0:NEAR_AT], proj[r])
            moving = second_stage()
            for copy in got_near:
                copy.wait_recv()
            for rows in tiles(EDGE):
                acc[rows, :] += dot(pick[rows, NEAR_AT:COARSE_AT], near[r].reshape(8 * BORDER, L))

        for d in (1, 2, 3):
            for k, (part, axis, offsets) in enumerate(PARTS):
                moving[k][d - 1].wait_recv()
                across.append(forward(part, axis, d))
        sent.extend(across)

        for rows in tiles(EDGE):
            acc[rows, :] += dot(pick[rows, COARSE_AT : COARSE_AT + 1024], coarse[r, 0].reshape(1024, L))

        for copy in across:
            copy.wait_recv()

        for rows in tiles(EDGE):
            before = acc[rows, :] + dot(pick[rows, COARSE_AT + 1024 : WIDE], coarse[r, 1].reshape(1024, L))
            result = norm(dot(hidden(before), w[OUT + 2 + 2 * r]), gains[2 + 2 * r : 3 + 2 * r, :])
            edges[rows, :] = (edges[rows, :].astype(F32) + result).astype(BF16)

        update = update_round(r)

    got_weights[3][0].wait()
    got_weights[3][1].wait()
    update(0, BORDER)
    proj[ROUNDS, 0:BORDER] = dot(mesh_now[0:BORDER], w[14]).astype(BF16)
    got_near = send_near(ROUNDS)
    update(BORDER, MESH)
    proj[ROUNDS, BORDER:MESH] = dot(mesh_now[BORDER:MESH], w[14]).astype(BF16)
    proj[ROUNDS, MESH : 2 * MESH] = jnp.zeros((MESH, L), BF16)

    square[...] = jnp.zeros_like(square)
    square[0:24] = m2g_src[...].astype(F32)
    columns(near_slot(square[...].astype(jnp.int32), 0, DEC_OWN), 24, 0)

    @pl.loop(0, ROWS)
    def _(t):
        to = pl.ds(pl.multiple_of(t * 128, 128), 128)
        for corner in range(3):
            one = short(acc[pl.ds(pl.multiple_of(corner * CELLS + t * 128, 128), 128), 0:128])
            for chunk in range(DEC_WIDE // 128):
                at = corner * DEC_WIDE + chunk * 128
                pick[to, at : at + 128] = ones_where_short(one == lanes + jnp.int16(chunk * 128))

    @pl.loop(0, CELLS // TILE)
    def _(t):
        rows = pl.ds(pl.multiple_of(t * TILE, TILE), TILE)
        base = dot(cells[rows, :], w[15])
        for corner in range(3):
            at = corner * DEC_WIDE
            to = pl.ds(pl.multiple_of(corner * CELLS + t * TILE, TILE), TILE)
            acc[to, :] = base + dot(pick[rows, at : at + DEC_OWN], proj[ROUNDS, 0:DEC_OWN])

    for copy in got_near:
        copy.wait_recv()

    @pl.loop(0, CELLS // TILE)
    def _(t):
        rows = pl.ds(pl.multiple_of(t * TILE, TILE), TILE)
        totals = jnp.zeros((TILE, L), F32)
        for corner in range(3):
            at = corner * DEC_WIDE
            to = pl.ds(pl.multiple_of(corner * CELLS + t * TILE, TILE), TILE)
            before = acc[to, :] + dot(
                pick[rows, at + DEC_OWN : at + DEC_WIDE], near[ROUNDS].reshape(8 * BORDER, L)
            )
            totals = totals + norm(dot(hidden(before), w[OUT + 6]), gains[6:7, :])
        out[rows, :] = new_nodes(cells[rows, :], dot(cells[rows, :], w[16]), totals, 17, 7)

    for copy in sent:
        copy.wait_send()


def on_device(
    grid_latent, mesh_latent, edge_latent, g2m_src, g2m_dst, g2m_count, mesh_src, mesh_dst, m2g_src,
    weights_in, weights_out, gains,
):
    anywhere = pl.BlockSpec(memory_space=pl.ANY)
    vmem = pl.BlockSpec(memory_space=pltpu.VMEM)
    result = pl.pallas_call(
        kernel,
        out_shape=jax.ShapeDtypeStruct((CELLS, L), BF16),
        in_specs=[anywhere, vmem, anywhere] + [vmem] * 6 + [anywhere, anywhere, vmem],
        out_specs=vmem,
        scratch_shapes=[
            pltpu.VMEM((26, L, L), BF16),
            pltpu.VMEM((GRID_ROWS, L), BF16),
            pltpu.VMEM((2048, L), BF16),
            pltpu.VMEM((EDGE, L), BF16),
            pltpu.VMEM((3 * CELLS, L), F32),
            pltpu.VMEM((EDGE, WIDE), BF16),
            pltpu.VMEM((MESH, EDGE + G2M), BF16),
            pltpu.VMEM((ROUNDS, 2, 4, 4, 4, COARSE, L), BF16),
            pltpu.VMEM((ROUNDS + 1, 8, BORDER, L), BF16),
            pltpu.VMEM((ROUNDS + 1, 2 * MESH, L), BF16),
            pltpu.VMEM((G2M, L), BF16),
            pltpu.VMEM((MESH, L), BF16),
            pltpu.VMEM((MESH, L), F32),
            pltpu.VMEM((2, 16, L), BF16),
            pltpu.VMEM((128, 128), F32),
            pltpu.SemaphoreType.DMA((10,)),
            pltpu.SemaphoreType.DMA((120,)),
            pltpu.SemaphoreType.DMA((120,)),
        ],
        compiler_params=pltpu.CompilerParams(
            collective_id=0, has_side_effects=True, vmem_limit_bytes=62 * 1024 * 1024
        ),
        cost_estimate=pl.CostEstimate(flops=40_000_000_000, bytes_accessed=20_000_000, transcendentals=10_000_000),
    )(
        grid_latent.reshape(CELLS, L), mesh_latent.reshape(MESH, L), edge_latent.reshape(EDGE, L),
        g2m_src.reshape(1, G2M), g2m_dst.reshape(1, G2M), g2m_count,
        mesh_src.reshape(1, EDGE), mesh_dst.reshape(1, EDGE), m2g_src.reshape(-1, 128),
        weights_in, weights_out, gains,
    )
    return result.reshape(grid_latent.shape)


def solution(mesh):
    placed = (
        P("lat", "lon", None),
        P("lat", "lon", None, None),
        P("lat", "lon", None, None),
        P("lat", "lon", None),
        P("lat", "lon", None),
        P("lat", "lon"),
        P("lat", "lon", None),
        P("lat", "lon", None),
        P(None, "lat", "lon"),
        P(),
        P(),
        P(),
    )
    return jax.shard_map(
        on_device, mesh=mesh, in_specs=placed, out_specs=P("lat", "lon", None), check_vma=False
    )
```

profile of v0, /device:TPU:0, one launch (start us, length us, event | category | flops | bytes accessed | tf_op | source)
XLA Modules:
  0.0 89.2 jit_solution(8591605314800910822)
XLA Ops:
  0.7 86.2 %shard_map.118 = bf16[1024,512]{1,0:T(8,128)(2,1)} custom-call(bf16[1024,512]{1,0:T(8,128)(2,1)} %bitcast.11, bf16[320,512]{1,0:T(8,128)(2,1)} %bitcast.12, bf16[2560,512]{1,0:T(8,128)(2,1)} %bitcast.10, s32[1,1536]{1,0:T(1,128)} %bitcast.16, s32[1,1536]{1,0:T(1,128)} %bitcast.17, s32[1,1]{1,0:T(1,128)S(6)} %copy.14.g2m_count, s32[1,2560]{1,0:T(1,128)} %bitcast.14, ...), custom_call_target="tpu_custom_call" | custom-call | flops 40000000000 | bytes 20000000 | tf_op jit(solution)/shard_map/pallas_call | solution.py:434
  86.9 2.3 %copy.15 = bf16[8,128,512]{2,1,0:T(8,128)(2,1)} copy(bf16[8,128,512]{2,1,0:T(8,128)(2,1)} %bitcast.9) | data formatting | bytes 2097152
where the time goes:
time: 90.6 us; the launch traced here: 89.2 us
  Pallas kernels  86.2 us (95%)
  local copies, waits for them, and re-layouts  2.26 us (2%)
    pallas_call x1, Pallas kernels, on_device(): pl.pallas_call(kernel, out_shape=jax.ShapeDtypeStruct((CELLS, L), BF16),...  86.2 us
    unnamed x1, local copies, waits for them, and re-layouts  2.26 us

commit v1 on v0

--- a/solution.py
+++ b/solution.py
@@ -347,9 +347,10 @@
                     + dot(pick[rows, NEAR_AT:COARSE_AT], near[r].reshape(8 * BORDER, L))
                 )
         else:
-            for rows in tiles(EDGE):
+            for t, rows in enumerate(tiles(EDGE)):
+                if t == 3:
+                    moving = second_stage()
                 acc[rows, :] = dot(edges[rows, :], w[first]) + dot(pick[rows, 0:NEAR_AT], proj[r])
-            moving = second_stage()
             for copy in got_near:
                 copy.wait_recv()
             for rows in tiles(EDGE):

time: 90.6 us -> 89.6 us (0.989)
  no operation moved by 1% of the time
where the time goes in v1:
time: 89.6 us; the launch traced here: 88.3 us
  Pallas kernels  85.4 us (95%)
  local copies, waits for them, and re-layouts  2.26 us (3%)
    pallas_call x1, Pallas kernels, on_device(): pl.pallas_call(kernel, out_shape=jax.ShapeDtypeStruct((CELLS, L), BF16),...  85.4 us
    unnamed x1, local copies, waits for them, and re-layouts  2.26 us

profile of v1, /device:TPU:0, one launch (start us, length us, event | category | flops | bytes accessed | tf_op | source)
XLA Modules:
  0.0 88.3 jit_solution(7852086893456310395)
XLA Ops:
  0.7 85.4 %shard_map.118 = bf16[1024,512]{1,0:T(8,128)(2,1)} custom-call(bf16[1024,512]{1,0:T(8,128)(2,1)} %bitcast.11, bf16[320,512]{1,0:T(8,128)(2,1)} %bitcast.12, bf16[2560,512]{1,0:T(8,128)(2,1)} %bitcast.10, s32[1,1536]{1,0:T(1,128)} %bitcast.16, s32[1,1536]{1,0:T(1,128)} %bitcast.17, s32[1,1]{1,0:T(1,128)S(6)} %copy.14.g2m_count, s32[1,2560]{1,0:T(1,128)} %bitcast.14, ...), custom_call_target="tpu_custom_call" | custom-call | flops 40000000000 | bytes 20000000 | tf_op jit(solution)/shard_map/pallas_call | solution.py:435
  86.1 2.3 %copy.15 = bf16[8,128,512]{2,1,0:T(8,128)(2,1)} copy(bf16[8,128,512]{2,1,0:T(8,128)(2,1)} %bitcast.9) | data formatting | bytes 2097152
